TPU v7x, 128 devices: a whole 4x4x4 slice. The times are simulated.
128 devices in a mesh: dp: 2 (over z_hi), seq: 16 (over z_lo, x, core), tensor: 4 (over y).
Axes of the slice: x: 4, y: 4, z: 4 (z_hi: 2, z_lo: 2; z = z_hi * 2 + z_lo), core: 2. Of those that a mesh axis runs over, the one named last changes fastest.
Arguments:
- queries: bfloat16 [8192, 8192], P(('dp', 'seq'), 'tensor'), parts along dimension 0, may hold values from -8 to 8
- keys: bfloat16 [2048, 8192], P(('dp', 'seq'), 'tensor'), parts along dimension 0, may hold values from -4 to 4
- values: bfloat16 [2048, 8192], P(('dp', 'seq'), 'tensor'), parts along dimension 0, may hold values from -6 to 6
- cotangent: bfloat16 [8192, 8192], P(('dp', 'seq'), 'tensor'), parts along dimension 0, may hold values from -6 to 6
- gate: float32 [8192], P('tensor'), may hold values from -1.5 to 1.5
- visible: int32 [64, 4], P(('dp', 'seq')), parts along dimension 0, may hold values from -1 to 15, as said below
Outputs:
- query_grad: bfloat16 [8192, 8192], P(('dp', 'seq'), 'tensor'), parts along dimension 0
- key_grad: bfloat16 [2048, 8192], P(('dp', 'seq'), 'tensor'), parts along dimension 0
- value_grad: bfloat16 [2048, 8192], P(('dp', 'seq'), 'tensor'), parts along dimension 0
- gate_grad: float32 [16384], P(('dp', 'tensor')), parts along dimension 0
There are 2 independent parts, one for each index of `dp`. A program takes and returns all parts, laid end to end along the dimension named above; an argument that names none is the same for every part. Nothing has to cross between parts.
Inputs may be any that keep to these rules, and one draw needn't show every extreme that they name: `visible`: row s lists the images that span s (tokens s * 128 to s * 128 + 127) may see, each at most once. A span on seq index r lists only images below (r + 1), and its slot 0 is image (r + 1) - 1. Unused slots hold -1 and follow the used ones; some span uses all 4 slots.
All inputs are finite; a program needn't handle non-finite values.
Results may differ from a plain program's by a relative error of at most 0.015.
Values may be sent and summed in bfloat16 or wider, within the bound.
A program may use at most 128 MiB of HBM per device.

v0:
```python
import functools

import jax
import jax.numpy as jnp
from jax import lax
from jax.experimental import pallas as pl
from jax.experimental.pallas import tpu as pltpu
from jax.sharding import PartitionSpec as P

MESH = pl.DeviceIdType.MESH
D = 128
LAT = 64
SPAN = 128
VIS = 4
CORE_HEADS = 8
N = 1
CHUNKS = CORE_HEADS // N
AHEAD = 2
IMAGES = 16
GATHER2, GATHER3, COMPUTE, BACK2, BACK3, LAST = 1, 2, 3, 5, 7, 9
NEG = -1e30
EXP2_SCALE = D**-0.5 * 1.4426950408889634
F32, BF16 = jnp.float32, jnp.bfloat16

(
    A_R, A_L, A_FR, A_FL, A_Z0, A_ZM, A_ZP, A_HR, A_HL,
    R_R, R_L, R_FR, R_FL, R_Z0, R_ZM, R_ZP, R_HR, R_HL,
) = range(18)
MESSAGES = 18
DQ, OUT_K, OUT_V, IN_K, IN_V = range(5)


def dot(a, b, ca, cb):
    return lax.dot_general(a, b, (((ca,), (cb,)), ((), ())), preferred_element_type=F32)


def kernel(
    q_ref, k_ref, v_ref, ct_ref, gate_hbm, vis_ref,
    qg_ref, kg_ref, vg_ref, gg_ref,
    qw, cw, kv, obuf, rbuf, kvw, sg_ref, low_ref, both_ref, dqs, fin, gpart, gall, gsum, first, gate_ref, vis_s, slot_s,
    ssem, rsem, hsend, hrecv, hout, lsem, lout, lfirst, esend, erecv, elocal, gsend, grecv, glast,
):
    seq = lax.axis_index("seq")
    c, k = lax.div(seq, 2), lax.rem(seq, 2)
    z, x = lax.div(c, 4), lax.rem(c, 4)
    xr, xl = lax.rem(x + 1, 4), lax.rem(x + 3, 4)
    xo = lax.rem(x + 2, 4)
    z0, z1 = z == 0, z == 1

    def at_chip(chip):
        return {"seq": chip * 2 + k}

    right_chip, left_chip, across_chip = z * 4 + xr, z * 4 + xl, (1 - z) * 4 + x
    right, left, across = at_chip(right_chip), at_chip(left_chip), at_chip(across_chip)
    partner = {"seq": c * 2 + (1 - k)}

    def send(idx, g, src, dst, dev):
        return pltpu.make_async_remote_copy(
            src_ref=src, dst_ref=dst, send_sem=ssem.at[idx], recv_sem=rsem.at[g, idx],
            device_id=dev, device_id_type=MESH,
        )

    def blk(buf, g, b):
        return buf.at[g, pl.ds(2 * b, 2)]

    def img(buf, g, b, half):
        return buf.at[g, pl.ds(2 * b + half, 1)]

    hi = z * 4

    def message(idx, g):
        own = blk(kv, g, c)
        if idx == A_R:
            return send(idx, g, own, own, right)
        if idx == A_L:
            return send(idx, g, own, own, left)
        if idx == A_FR:
            b = blk(kv, g, hi + xl)
            return send(idx, g, b, b, right)
        if idx == A_FL:
            b = blk(kv, g, hi + xr)
            return send(idx, g, b, b, left)
        if idx == A_Z0:
            return send(idx, g, own, own, across)
        if idx == A_ZM:
            b = blk(kv, g, xl)
            return send(idx, g, b, b, across)
        if idx == A_ZP:
            b = blk(kv, g, xr)
            return send(idx, g, b, b, across)
        if idx == A_HR:
            b = img(kv, g, xl, 0)
            return send(idx, g, b, b, right)
        if idx == A_HL:
            b = img(kv, g, xr, 1)
            return send(idx, g, b, b, left)
        if idx == R_R:
            return send(idx, g, blk(obuf, g, hi + xl), rbuf.at[g, 0], left)
        if idx == R_L:
            return send(idx, g, blk(obuf, g, hi + xr), rbuf.at[g, 1], right)
        if idx == R_FR:
            return send(idx, g, blk(obuf, g, hi + xo), rbuf.at[g, 2], left)
        if idx == R_FL:
            return send(idx, g, blk(obuf, g, hi + xo), rbuf.at[g, 3], right)
        if idx == R_Z0:
            return send(idx, g, blk(obuf, g, x), rbuf.at[g, 4], across)
        if idx == R_ZM:
            return send(idx, g, blk(obuf, g, xl), rbuf.at[g, 5], across)
        if idx == R_ZP:
            return send(idx, g, blk(obuf, g, xr), rbuf.at[g, 6], across)
        if idx == R_HR:
            return send(idx, g, img(obuf, g, xo, 0), rbuf.at[g, 7, pl.ds(0, 1)], left)
        if idx == R_HL:
            return send(idx, g, img(obuf, g, xo, 1), rbuf.at[g, 7, pl.ds(1, 1)], right)
        raise ValueError(idx)

    def swap(idx, h, src, dst):
        return pltpu.make_async_remote_copy(
            src_ref=src, dst_ref=dst, send_sem=hsend.at[idx], recv_sem=hrecv.at[h, idx - IN_K],
            device_id=partner, device_id_type=MESH,
        )

    def swap_all(idx, src, dst):
        return pltpu.make_async_remote_copy(
            src_ref=src, dst_ref=dst, send_sem=hsend.at[idx], recv_sem=hout.at[idx],
            device_id=partner, device_id_type=MESH,
        )

    def head_message(idx, h):
        g, n = lax.div(h, N), lax.rem(h, N)
        theirs = head_cols(1 - k, h)
        if idx == IN_K:
            return swap(idx, h, k_ref.at[:, theirs], kv.at[g, seq, 0, n])
        return swap(idx, h, v_ref.at[:, theirs], kv.at[g, seq, 1, n])

    def head_got(idx, h, dst):
        swap(idx, h, dst, dst).wait_recv()

    def head_cols(core, h):
        return pl.ds(pl.multiple_of((core * CORE_HEADS + h) * D, D), D)

    def got(idx, g, dst):
        send(idx, g, dst, dst, partner).wait_recv()

    def own_copies(h):
        g, n = lax.div(h, N), lax.rem(h, N)
        mine = head_cols(k, h)
        return (
            pltpu.make_async_copy(k_ref.at[:, mine], kv.at[g, seq, 0, n], lsem.at[h, 0]),
            pltpu.make_async_copy(v_ref.at[:, mine], kv.at[g, seq, 1, n], lsem.at[h, 1]),
        )

    half_width = CORE_HEADS * D
    half_cols = pl.ds(pl.multiple_of(k * half_width, half_width), half_width)
    their_cols = pl.ds(pl.multiple_of((1 - k) * half_width, half_width), half_width)
    my_rows, their_rows = pl.ds(k * 256, 256), pl.ds((1 - k) * 256, 256)

    def result_copies():
        results = ((1, fin.at[k, 0], kg_ref), (2, fin.at[k, 1], vg_ref))
        return [
            pltpu.make_async_copy(src, ref.at[:, half_cols], lout.at[i]) for i, src, ref in results
        ] + [
            swap_all(OUT_K, fin.at[1 - k, 0], kg_ref.at[:, half_cols]),
            swap_all(OUT_V, fin.at[1 - k, 1], vg_ref.at[:, half_cols]),
        ]

    def query_copies():
        return [
            pltpu.make_async_copy(dqs.at[my_rows], qg_ref.at[:, half_cols], lout.at[0]),
            swap_all(DQ, dqs.at[their_rows], qg_ref.at[:, half_cols]),
        ]

    def early(i, src, dst):
        return pltpu.make_async_remote_copy(
            src_ref=src, dst_ref=dst, send_sem=esend.at[i], recv_sem=erecv.at[i],
            device_id=partner, device_id_type=MESH,
        )

    swaps = [
        early(0, vis_ref, vis_s.at[k]),
        early(1, q_ref.at[:, their_cols], qw.at[my_rows]),
        early(2, ct_ref.at[:, their_cols], cw.at[my_rows]),
    ]
    keeps = [
        pltpu.make_async_copy(vis_ref, vis_s.at[k], elocal.at[0]),
        pltpu.make_async_copy(q_ref.at[:, half_cols], qw.at[my_rows], elocal.at[1]),
        pltpu.make_async_copy(ct_ref.at[:, half_cols], cw.at[my_rows], elocal.at[2]),
        pltpu.make_async_copy(gate_hbm, gate_ref, elocal.at[3]),
    ]

    first_cols = head_cols(1 - k, 0)
    first_copies = [
        pltpu.make_async_copy(k_ref.at[:, first_cols], first.at[0, 0, 0], lfirst.at[0]),
        pltpu.make_async_copy(v_ref.at[:, first_cols], first.at[0, 1, 0], lfirst.at[1]),
    ]

    def first_messages(idx, chip):
        mine = kv.at[0, pl.ds(seq, 1)]
        return [
            pltpu.make_async_remote_copy(
                src_ref=src, dst_ref=mine, send_sem=ssem.at[idx], recv_sem=rsem.at[0, idx],
                device_id={"seq": chip * 2 + core}, device_id_type=MESH,
            )
            for src, core in ((mine, k), (first, 1 - k))
        ]

    def send_first():
        for copy in (*own_copies(0), *first_copies):
            copy.wait()

        @pl.when(jnp.logical_or(z0, x < 3))
        def _():
            for copy in first_messages(A_R, right_chip):
                copy.start()

        @pl.when(jnp.logical_or(z0, x == 0))
        def _():
            for copy in first_messages(A_L, left_chip):
                copy.start()

        @pl.when(z0)
        def _():
            for copy in first_messages(A_Z0, across_chip):
                copy.start()

    for copy in first_copies:
        copy.start()
    for h in range(AHEAD):
        for copy in own_copies(h):
            copy.start()

    for copy in keeps:
        copy.start()

    barrier = pltpu.get_barrier_semaphore()
    greeted = [{"seq": chip * 2 + m} for chip in (right_chip, left_chip, across_chip) for m in (0, 1)]
    for device in greeted + [partner]:
        pl.semaphore_signal(barrier, inc=1, device_id=device, device_id_type=MESH)
    pl.semaphore_wait(barrier, 7)

    send_first()

    for h in range(AHEAD):
        head_message(IN_K, h).start()
        head_message(IN_V, h).start()

    for copy in swaps:
        copy.start()

    sg_ref[:, VIS] = jnp.zeros((4, LAT, SPAN), BF16)
    low_ref[:, VIS] = jnp.zeros((4, LAT, SPAN), BF16)

    def prepare():
        for copy in keeps:
            copy.wait()
        for copy in swaps:
            copy.wait()

        @pl.loop(0, IMAGES)
        def _(i):
            for s in range(4):
                slot = jnp.int32(VIS)
                for v in range(VIS):
                    slot = jnp.where(vis_s[s // 2, s % 2, v] == i, v, slot)
                slot_s[s, i] = slot

    def when(cond):
        return pl.when(cond)

    def span_work(h):
        cols = pl.ds(pl.multiple_of(h * D, D), D)
        kvw[...] = kv[h, :, :, 0]
        tanh_gate = jnp.tanh(gate_ref[pl.ds(k * CORE_HEADS + h, 1), :])
        q_all = qw[:, cols]
        ct_all = cw[:, cols]
        go_all = (tanh_gate * ct_all.astype(F32)).astype(BF16)
        both_ref[:, :D] = go_all
        both_ref[:, D:] = ct_all
        spans = range(4)
        listed = [[vis_s[s // 2, s % 2, v] for v in range(VIS)] for s in spans]
        ids = [[jnp.maximum(i, 0) for i in row] for row in listed]
        q = [q_all[s * SPAN : (s + 1) * SPAN] for s in spans]
        go = [go_all[s * SPAN : (s + 1) * SPAN] for s in spans]
        kl = [jnp.concatenate([kvw[i, 0] for i in ids[s]], axis=0) for s in spans]
        vl = [jnp.concatenate([kvw[i, 1] for i in ids[s]], axis=0) for s in spans]
        raw = [dot(kl[s], q[s], 1, 1) for s in spans]
        wg = [dot(vl[s], go[s], 1, 1) for s in spans]
        p, low, sg = [], [], []
        for s in spans:
            rows = [raw[s][:LAT] * EXP2_SCALE]
            for v in range(1, VIS):
                bias = jnp.where(listed[s][v] >= 0, 0.0, NEG).astype(F32)
                rows.append(raw[s][v * LAT : (v + 1) * LAT] * EXP2_SCALE + bias)
            sc = jnp.concatenate(rows, axis=0)
            e = jnp.exp2(sc - jnp.max(sc, axis=0, keepdims=True))
            p.append(e * (1.0 / jnp.sum(e, axis=0, keepdims=True)))
            low.append(p[s].astype(BF16))
        for s in spans:
            dots = jnp.sum(low[s].astype(F32) * wg[s], axis=0, keepdims=True)
            sg.append((p[s] * (wg[s] - dots)).astype(BF16))
        for s in spans:
            low_ref[s, pl.ds(0, VIS)] = low[s].reshape(VIS, LAT, SPAN)
            sg_ref[s, pl.ds(0, VIS)] = sg[s].reshape(VIS, LAT, SPAN)
        dq = [dot(sg[s], kl[s], 0, 0) * (D**-0.5) for s in spans]
        for s in spans:
            dqs[pl.ds(s * SPAN, SPAN), cols] = dq[s].astype(BF16)

    def products(g):
        tanh_gate = jnp.tanh(gate_ref[pl.ds(k * CORE_HEADS + g, 1), :])
        q_all = qw[:, pl.ds(pl.multiple_of(g * D, D), D)]
        both = both_ref[...]

        def images(count):
            left, low_left, vals = [], [], []
            for i in range(count):
                slots = [slot_s[s, i] for s in range(4)]
                left.append(jnp.concatenate([sg_ref[s, slots[s]] for s in range(4)], axis=1))
                low_left.append(jnp.concatenate([low_ref[s, slots[s]] for s in range(4)], axis=1))
                vals.append(jnp.where(i < 2 * (c + 1), kvw[i, 1].astype(F32), 0.0))
            dk = dot(jnp.concatenate(left, axis=0), q_all, 1, 0) * (D**-0.5)
            obuf[g, pl.ds(0, count), 0, 0] = dk.reshape(count, LAT, D).astype(BF16)
            vw = dot(jnp.concatenate(low_left, axis=0), both, 1, 0)
            obuf[g, pl.ds(0, count), 1, 0] = vw[:, :D].reshape(count, LAT, D).astype(BF16)
            vals = jnp.concatenate(vals, axis=0)
            gate_sum = jnp.sum(vals * vw[:, D:], axis=0, keepdims=True)
            gpart[pl.ds(g, 1), :] = gate_sum * (1.0 - tanh_gate * tanh_gate)

        @when(z0)
        def _():
            images(8)

        @when(z1)
        def _():
            images(16)

    def add(g, b, slot):
        rows = pl.ds(2 * b, 2)
        obuf[g, rows] = (obuf[g, rows].astype(F32) + rbuf[g, slot].astype(F32)).astype(BF16)

    def swapped(g):
        other = c * 2 + (1 - k)
        head_got(IN_K, g, kv.at[g, other, 0, 0])
        head_got(IN_V, g, kv.at[g, other, 1, 0])

    def gather1(g):
        for copy in own_copies(g):
            copy.wait()
        swapped(g)

        @when(jnp.logical_or(z0, x < 3))
        def _():
            message(A_R, g).start()

        @when(jnp.logical_or(z0, x == 0))
        def _():
            message(A_L, g).start()

    def gather2(g):
        @when(jnp.logical_or(z0, x > 0))
        def _():
            got(A_R, g, blk(kv, g, hi + xl))

        @when(z0)
        def _():
            message(A_ZM, g).start()
            got(A_L, g, blk(kv, g, hi + xr))
            message(A_ZP, g).start()

    def gather_own(g):
        @when(z0)
        def _():
            message(A_Z0, g).start()

    def gather_forward(g):
        @when(jnp.logical_or(x == 1, jnp.logical_and(z1, x == 2)))
        def _():
            message(A_FR, g).start()

        @when(jnp.logical_and(z0, x == 0))
        def _():
            message(A_FL, g).start()

    def gather3(g):
        @when(z1)
        def _():
            got(A_ZM, g, blk(kv, g, xl))
            message(A_HR, g).start()
            got(A_ZP, g, blk(kv, g, xr))
            message(A_HL, g).start()

    def gather4(g):
        @when(z1)
        def _():
            got(A_Z0, g, blk(kv, g, x))
            got(A_HR, g, img(kv, g, xo, 0))
            got(A_HL, g, img(kv, g, xo, 1))

        @when(jnp.logical_or(x == 2, jnp.logical_and(z1, x == 3)))
        def _():
            got(A_FR, g, blk(kv, g, hi + xo))

        @when(jnp.logical_and(z0, x == 3))
        def _():
            got(A_FL, g, blk(kv, g, xo))

        @when(jnp.logical_and(z1, x == 3))
        def _():
            got(A_L, g, blk(kv, g, 4))

    def back1(g):
        @when(z1)
        def _():
            message(R_HR, g).start()
            message(R_HL, g).start()
            message(R_Z0, g).start()

        @when(jnp.logical_or(x == 2, jnp.logical_and(z1, x == 3)))
        def _():
            message(R_FR, g).start()

        @when(jnp.logical_and(z0, x == 3))
        def _():
            message(R_FL, g).start()

        @when(jnp.logical_and(z1, x == 3))
        def _():
            message(R_L, g).start()

    def back2(g):
        @when(z1)
        def _():
            got(R_HR, g, rbuf.at[g, 7, pl.ds(0, 1)])
            row = 2 * xl
            obuf[g, row] = (obuf[g, row].astype(F32) + rbuf[g, 7, 0].astype(F32)).astype(BF16)
            message(R_ZM, g).start()
            got(R_HL, g, rbuf.at[g, 7, pl.ds(1, 1)])
            row = 2 * xr + 1
            obuf[g, row] = (obuf[g, row].astype(F32) + rbuf[g, 7, 1].astype(F32)).astype(BF16)
            message(R_ZP, g).start()

            @when(jnp.logical_or(x == 1, x == 2))
            def _():
                got(R_FR, g, rbuf.at[g, 2])
                add(g, 4 + xl, 2)

            @when(x > 0)
            def _():
                message(R_R, g).start()

    def back3(g):
        @when(z0)
        def _():
            @when(x == 1)
            def _():
                got(R_FR, g, rbuf.at[g, 2])
                add(g, xl, 2)

            @when(x == 0)
            def _():
                got(R_FL, g, rbuf.at[g, 3])
                add(g, xr, 3)

            got(R_ZM, g, rbuf.at[g, 5])
            add(g, xl, 5)
            message(R_R, g).start()
            got(R_ZP, g, rbuf.at[g, 6])
            add(g, xr, 6)
            message(R_L, g).start()

    def back4(g):
        own = pl.ds(2 * c, 2)

        def finish(slots):
            total = obuf[g, own].astype(F32)
            for slot in slots:
                total += rbuf[g, slot].astype(F32)
            fin[:, :, :, pl.ds(pl.multiple_of(g * D, D), D)] = total[:, :, 0].astype(BF16)

        @when(z0)
        def _():
            got(R_Z0, g, rbuf.at[g, 4])
            got(R_R, g, rbuf.at[g, 0])
            got(R_L, g, rbuf.at[g, 1])
            finish((4, 0, 1))

        @when(z1)
        def _():
            @when(x < 3)
            def _():
                got(R_R, g, rbuf.at[g, 0])

            @when(x == 0)
            def _():
                got(R_L, g, rbuf.at[g, 1])
                finish((0, 1))

            @when(jnp.logical_or(x == 1, x == 2))
            def _():
                finish((0,))

            @when(x == 3)
            def _():
                finish(())

    odd = lax.rem(x, 2)
    pairs = (
        across,
        at_chip(z * 4 + x + 1 - 2 * odd),
        at_chip(z * 4 + lax.rem(x + 3 + 2 * odd, 4)),
    )

    def gate_step(i):
        return pltpu.make_async_remote_copy(
            src_ref=gsum.at[i], dst_ref=gall.at[i], send_sem=gsend.at[i], recv_sem=grecv.at[i],
            device_id=pairs[i], device_id_type=MESH,
        )

    gate_local = pltpu.make_async_copy(gsum.at[3], gg_ref.at[k], glast.at[0])
    gate_remote = pltpu.make_async_remote_copy(
        src_ref=gsum.at[3], dst_ref=gg_ref.at[k], send_sem=glast.at[1], recv_sem=glast.at[2],
        device_id=partner, device_id_type=MESH,
    )

    @pl.loop(0, CHUNKS + LAST)
    def _(t):
        def stage(offset, run, first=0):
            @when(jnp.logical_and(t >= offset + first, t < CHUNKS + offset))
            def _():
                run(t - offset)

        @when(t < CHUNKS - AHEAD)
        def _():
            for copy in own_copies(t + AHEAD):
                copy.start()
            head_message(IN_K, t + AHEAD).start()
            head_message(IN_V, t + AHEAD).start()

        stage(0, gather1, 1)
        stage(GATHER2, gather2)
        stage(0, gather_own, 1)
        stage(GATHER2, gather_forward)
        stage(BACK2, back2)
        stage(BACK3, back3)
        stage(LAST, back4)

        @when(t == COMPUTE - 1)
        def _():
            prepare()
            swapped(0)

        stage(COMPUTE, gather4)
        stage(COMPUTE, span_work)
        stage(GATHER3, gather3)
        stage(COMPUTE, products)
        stage(COMPUTE, back1)

        @when(t == CHUNKS + COMPUTE - 1)
        def _():
            for copy in query_copies():
                copy.start()
            gsum[0] = gpart[...]
            gate_step(0).start()

        for i in range(3):

            @when(t == CHUNKS + COMPUTE + i)
            def _():
                gate_step(i).wait_recv()
                gsum[i + 1] = gsum[i] + gall[i]
                if i < 2:
                    gate_step(i + 1).start()
                else:
                    gate_local.start()
                    gate_remote.start()

    for copy in result_copies():
        copy.start()
    for i in range(3):
        gate_step(i).wait_send()

    def done(idx):
        half = idx in (A_HR, A_HL, R_HR, R_HL)
        sent = kv.at[:, pl.ds(0, 1 if half else 2)]
        pltpu.make_async_remote_copy(
            src_ref=sent, dst_ref=sent, send_sem=ssem.at[idx], recv_sem=rsem.at[0, idx],
            device_id=partner, device_id_type=MESH,
        ).wait_send()

    @when(z0)
    def _():
        for idx in (A_Z0, A_ZM, A_ZP):
            done(idx)

    @when(z1)
    def _():
        for idx in (A_HR, A_HL, R_HR, R_HL, R_Z0, R_ZM, R_ZP):
            done(idx)

    @when(jnp.logical_or(z0, x < 3))
    def _():
        done(A_R)

    @when(jnp.logical_or(z0, x == 0))
    def _():
        done(A_L)

    @when(jnp.logical_or(x == 1, jnp.logical_and(z1, x == 2)))
    def _():
        done(A_FR)

    @when(jnp.logical_and(z0, x == 0))
    def _():
        done(A_FL)

    @when(jnp.logical_or(x == 2, jnp.logical_and(z1, x == 3)))
    def _():
        done(R_FR)

    @when(jnp.logical_and(z0, x == 3))
    def _():
        done(R_FL)

    @when(jnp.logical_or(z0, x == 3))
    def _():
        done(R_L)

    @when(jnp.logical_or(z0, x > 0))
    def _():
        done(R_R)

    swap_all(DQ, dqs.at[their_rows], qg_ref.at[:, their_cols]).wait_send()
    swap_all(OUT_K, fin.at[1 - k, 0], kg_ref.at[:, their_cols]).wait_send()
    swap_all(OUT_V, fin.at[1 - k, 1], vg_ref.at[:, their_cols]).wait_send()
    swap_all(IN_K, k_ref.at[:, their_cols], kg_ref.at[:, their_cols]).wait_send()
    swap_all(IN_V, v_ref.at[:, their_cols], vg_ref.at[:, their_cols]).wait_send()
    for idx, ref in ((DQ, qg_ref), (OUT_K, kg_ref), (OUT_V, vg_ref)):
        swap_all(idx, ref.at[:, their_cols], ref.at[:, their_cols]).wait_recv()
    pltpu.make_async_copy(qg_ref.at[:, half_cols], qg_ref.at[:, half_cols], lout.at[0]).wait()
    pltpu.make_async_copy(kg_ref.at[:, half_cols], kg_ref.at[:, half_cols], lout.at[1]).wait()
    pltpu.make_async_copy(vg_ref.at[:, half_cols], vg_ref.at[:, half_cols], lout.at[2]).wait()

    gate_local.wait()
    gate_remote.wait_send()
    pltpu.make_async_remote_copy(
        src_ref=gsum.at[3], dst_ref=gg_ref.at[1 - k], send_sem=glast.at[1], recv_sem=glast.at[2],
        device_id=partner, device_id_type=MESH,
    ).wait_recv()


def place(a0, a1, a2, a3, b0, b1, b2, b3, m0, m1, m2, m3, sem):
    held = (m0, m1, m2, m3)
    into = [
        pltpu.make_async_copy(a, m, sem.at[0, i]) for i, (a, m) in enumerate(zip((a0, a1, a2, a3), held))
    ]
    out = [
        pltpu.make_async_copy(m, b, sem.at[1, i]) for i, (m, b) in enumerate(zip(held, (b0, b1, b2, b3)))
    ]
    for copy in into:
        copy.start()
    for copy, after in zip(into, out):
        copy.wait()
        after.start()
    for copy in out:
        copy.wait()


def shards(queries, keys, values, cotangent, gate, visible):
    tokens, width = queries.shape
    half = width // 2
    any_spec = pl.BlockSpec(memory_space=pl.ANY)
    hbm_spec = pl.BlockSpec(memory_space=pltpu.HBM)
    dma = pltpu.SemaphoreType.DMA
    out_shape = (
        jax.ShapeDtypeStruct((tokens, width), BF16),
        jax.ShapeDtypeStruct((LAT, width), BF16),
        jax.ShapeDtypeStruct((LAT, width), BF16),
        jax.ShapeDtypeStruct((2, CORE_HEADS, D), F32),
    )
    results = pl.pallas_call(
        kernel,
        out_shape=out_shape,
        in_specs=[hbm_spec] * 6,
        out_specs=(any_spec,) * 4,
        scratch_shapes=[
            pltpu.VMEM((2 * tokens, half), BF16),
            pltpu.VMEM((2 * tokens, half), BF16),
            pltpu.VMEM((CHUNKS, IMAGES, 2, N, LAT, D), BF16),
            pltpu.VMEM((CHUNKS, IMAGES, 2, N, LAT, D), BF16),
            pltpu.VMEM((CHUNKS, 8, 2, 2, N, LAT, D), BF16),
            pltpu.VMEM((IMAGES, 2, LAT, D), BF16),
            pltpu.VMEM((4, VIS + 1, LAT, SPAN), BF16),
            pltpu.VMEM((4, VIS + 1, LAT, SPAN), BF16),
            pltpu.VMEM((2 * tokens, 2 * D), BF16),
            pltpu.VMEM((2 * tokens, half), BF16),
            pltpu.VMEM((2, 2, LAT, half), BF16),
            pltpu.VMEM((CORE_HEADS, D), F32),
            pltpu.VMEM((3, CORE_HEADS, D), F32),
            pltpu.VMEM((4, CORE_HEADS, D), F32),
            pltpu.VMEM((1, 2, N, LAT, D), BF16),
            pltpu.VMEM((2 * CORE_HEADS, D), F32),
            pltpu.SMEM((2, 2, VIS), jnp.int32),
            pltpu.SMEM((4, IMAGES), jnp.int32),
            dma((MESSAGES,)),
            dma((CHUNKS, MESSAGES)),
            dma((5,)),
            dma((CORE_HEADS, 2)),
            dma((3,)),
            dma((CORE_HEADS, 2)),
            dma((3,)),
            dma((2,)),
            dma((3,)),
            dma((3,)),
            dma((4,)),
            dma((3,)),
            dma((3,)),
            dma((3,)),
        ],
        compiler_params=pltpu.CompilerParams(
            collective_id=0, has_side_effects=True, vmem_limit_bytes=63 * 1024 * 1024
        ),
        name="cross_attention_backward",
    )(queries, keys, values, cotangent, gate.reshape(2 * CORE_HEADS, D), visible)
    query_grad, key_grad, value_grad, gate_grad = pl.pallas_call(
        place,
        out_shape=out_shape,
        in_specs=[any_spec] * 4,
        out_specs=(hbm_spec,) * 4,
        scratch_shapes=[pltpu.VMEM(o.shape, o.dtype) for o in out_shape] + [dma((2, 4))],
        compiler_params=pltpu.CompilerParams(vmem_limit_bytes=63 * 1024 * 1024),
        name="place_results",
    )(*results)
    return query_grad, key_grad, value_grad, gate_grad.reshape(width)


def solution(mesh):
    placed = (
        P(("dp", "seq"), "tensor"),
        P(("dp", "seq"), "tensor"),
        P(("dp", "seq"), "tensor"),
        P(("dp", "seq"), "tensor"),
        P("tensor"),
        P(("dp", "seq"), None),
    )
    return jax.shard_map(
        shards,
        mesh=mesh,
        in_specs=placed,
        out_specs=(
            P(("dp", "seq"), "tensor"),
            P(("dp", "seq"), "tensor"),
            P(("dp", "seq"), "tensor"),
            P(("dp", "tensor")),
        ),
        check_vma=False,
    )
```

profile of v0, /device:TPU:1, one launch (start us, length us, event | category | flops | bytes accessed | tf_op | source)
XLA Modules:
  0.0 68.4 jit_solution(16736507669923088758)
XLA Ops:
  0.6 65.4 %cross_attention_backward.1 = (bf16[256,2048]{1,0:T(8,128)(2,1)}, bf16[64,2048]{1,0:T(8,128)(2,1)}, bf16[64,2048]{1,0:T(8,128)(2,1)}, f32[2,8,128]{2,1,0:T(8,128)}) custom-call(bf16[256,2048]{1,0:T(8,128)(2,1)} %q_ref.1, bf16[64,2048]{1,0:T(8,128)(2,1)} %k_ref.1, bf16[64,2048]{1,0:T(8,128)(2,1)} %v_ref.1, bf16[256,2048]{1,0:T(8,128)(2,1)} %ct_ref.1, ...), custom_call_target="tpu_custom_call" | custom-call | tf_op jit(solution)/shard_map/cross_attention_backward/pallas_call | solution.py:679
  66.0 2.4 %place_results.1 = (bf16[256,2048]{1,0:T(8,128)(2,1)}, bf16[64,2048]{1,0:T(8,128)(2,1)}, bf16[64,2048]{1,0:T(8,128)(2,1)}, f32[2,8,128]{2,1,0:T(8,128)}) custom-call(bf16[256,2048]{1,0:T(8,128)(2,1)} %get-tuple-element.12.a0, bf16[64,2048]{1,0:T(8,128)(2,1)} %get-tuple-element.13.a1, bf16[64,2048]{1,0:T(8,128)(2,1)} %get-tuple-element.14.a2, ...), custom_call_target="tpu_custom_call" | custom-call | tf_op jit(solution)/shard_map/place_results/pallas_call | solution.py:723
where the time goes:
time: 68.6 us; the launch traced here: 68.4 us
  Pallas kernels  67.8 us (99%)
    pallas_call x1, Pallas kernels, shards(): pl.pallas_call(kernel, out_shape=out_shape, in_specs=[hbm_spec] * 6, out_...  65.4 us
    pallas_call x1, Pallas kernels, shards(): pl.pallas_call(place, out_shape=out_shape, in_specs=[any_spec] * 4, out_s...  2.43 us

commit v1 on v0

--- a/solution.py
+++ b/solution.py
@@ -127,7 +127,7 @@
         )
 
     def head_message(idx, h):
-        g, n = lax.div(h, N), lax.rem(h, N)
+        g, n = h, 0
         theirs = head_cols(1 - k, h)
         if idx == IN_K:
             return swap(idx, h, k_ref.at[:, theirs], kv.at[g, seq, 0, n])
@@ -143,7 +143,7 @@
         send(idx, g, dst, dst, partner).wait_recv()
 
     def own_copies(h):
-        g, n = lax.div(h, N), lax.rem(h, N)
+        g, n = h, 0
         mine = head_cols(k, h)
         return (
             pltpu.make_async_copy(k_ref.at[:, mine], kv.at[g, seq, 0, n], lsem.at[h, 0]),
@@ -521,20 +521,31 @@
         device_id=partner, device_id_type=MESH,
     )
 
-    @pl.loop(0, CHUNKS + LAST)
-    def _(t):
+    def iteration(t):
+        fixed = isinstance(t, int)
+
         def stage(offset, run, first=0):
-            @when(jnp.logical_and(t >= offset + first, t < CHUNKS + offset))
-            def _():
+            if fixed:
+                if offset + first <= t < CHUNKS + offset:
+                    run(t - offset)
+                return
+            conditions = []
+            if offset + first > COMPUTE:
+                conditions.append(t >= offset + first)
+            if offset < COMPUTE:
+                conditions.append(t < CHUNKS + offset)
+            if not conditions:
                 run(t - offset)
-
-        @when(t < CHUNKS - AHEAD)
-        def _():
-            for copy in own_copies(t + AHEAD):
+            else:
+                pl.when(functools.reduce(jnp.logical_and, conditions))(lambda: run(t - offset))
+
+        def fetch(g):
+            for copy in own_copies(g):
                 copy.start()
-            head_message(IN_K, t + AHEAD).start()
-            head_message(IN_V, t + AHEAD).start()
-
+            head_message(IN_K, g).start()
+            head_message(IN_V, g).start()
+
+        stage(-AHEAD, lambda g: fetch(g))
         stage(0, gather1, 1)
         stage(GATHER2, gather2)
         stage(0, gather_own, 1)
@@ -542,36 +553,38 @@
         stage(BACK2, back2)
         stage(BACK3, back3)
         stage(LAST, back4)
-
-        @when(t == COMPUTE - 1)
-        def _():
-            prepare()
-            swapped(0)
-
-        stage(COMPUTE, gather4)
-        stage(COMPUTE, span_work)
+        if not fixed:
+            gather4(t - COMPUTE)
+            span_work(t - COMPUTE)
         stage(GATHER3, gather3)
-        stage(COMPUTE, products)
-        stage(COMPUTE, back1)
-
-        @when(t == CHUNKS + COMPUTE - 1)
-        def _():
-            for copy in query_copies():
-                copy.start()
-            gsum[0] = gpart[...]
-            gate_step(0).start()
-
-        for i in range(3):
-
-            @when(t == CHUNKS + COMPUTE + i)
-            def _():
-                gate_step(i).wait_recv()
-                gsum[i + 1] = gsum[i] + gall[i]
-                if i < 2:
-                    gate_step(i + 1).start()
-                else:
-                    gate_local.start()
-                    gate_remote.start()
+        if not fixed:
+            products(t - COMPUTE)
+            back1(t - COMPUTE)
+
+    for t in range(COMPUTE - 1):
+        iteration(t)
+    prepare()
+    iteration(COMPUTE - 1)
+    swapped(0)
+
+    @pl.loop(COMPUTE, COMPUTE + CHUNKS)
+    def _(t):
+        iteration(t)
+
+    for copy in query_copies():
+        copy.start()
+    gsum[0] = gpart[...]
+    gate_step(0).start()
+    for i in range(LAST - COMPUTE):
+        iteration(COMPUTE + CHUNKS + i)
+        if i < 3:
+            gate_step(i).wait_recv()
+            gsum[i + 1] = gsum[i] + gall[i]
+            if i < 2:
+                gate_step(i + 1).start()
+            else:
+                gate_local.start()
+                gate_remote.start()
 
     for copy in result_copies():
         copy.start()

time: 68.6 us -> 68.5 us (level)
  no operation moved by 1% of the time
where the time goes in v1:
time: 68.5 us; the launch traced here: 68.4 us
  Pallas kernels  67.7 us (99%)
    pallas_call x1, Pallas kernels, shards(): pl.pallas_call(kernel, out_shape=out_shape, in_specs=[hbm_spec] * 6, out_...  65.3 us
    pallas_call x1, Pallas kernels, shards(): pl.pallas_call(place, out_shape=out_shape, in_specs=[any_spec] * 4, out_s...  2.43 us

profile of v1, /device:TPU:1, one launch (start us, length us, event | category | flops | bytes accessed | tf_op | source)
XLA Modules:
  0.0 68.4 jit_solution(4717061890386081821)
XLA Ops:
  0.6 65.3 %cross_attention_backward.1 = (bf16[256,2048]{1,0:T(8,128)(2,1)}, bf16[64,2048]{1,0:T(8,128)(2,1)}, bf16[64,2048]{1,0:T(8,128)(2,1)}, f32[2,8,128]{2,1,0:T(8,128)}) custom-call(bf16[256,2048]{1,0:T(8,128)(2,1)} %q_ref.1, bf16[64,2048]{1,0:T(8,128)(2,1)} %k_ref.1, bf16[64,2048]{1,0:T(8,128)(2,1)} %v_ref.1, bf16[256,2048]{1,0:T(8,128)(2,1)} %ct_ref.1, ...), custom_call_target="tpu_custom_call" | custom-call | tf_op jit(solution)/shard_map/cross_attention_backward/pallas_call | solution.py:692
  65.9 2.4 %place_results.1 = (bf16[256,2048]{1,0:T(8,128)(2,1)}, bf16[64,2048]{1,0:T(8,128)(2,1)}, bf16[64,2048]{1,0:T(8,128)(2,1)}, f32[2,8,128]{2,1,0:T(8,128)}) custom-call(bf16[256,2048]{1,0:T(8,128)(2,1)} %get-tuple-element.12.a0, bf16[64,2048]{1,0:T(8,128)(2,1)} %get-tuple-element.13.a1, bf16[64,2048]{1,0:T(8,128)(2,1)} %get-tuple-element.14.a2, ...), custom_call_target="tpu_custom_call" | custom-call | tf_op jit(solution)/shard_map/place_results/pallas_call | solution.py:736

commit v2 on v1

--- a/solution.py
+++ b/solution.py
@@ -27,7 +27,7 @@
     R_R, R_L, R_FR, R_FL, R_Z0, R_ZM, R_ZP, R_HR, R_HL,
 ) = range(18)
 MESSAGES = 18
-DQ, OUT_K, OUT_V, IN_K, IN_V = range(5)
+DQ, OUT, IN_K, IN_V, IN_Q, IN_C = range(6)
 
 
 def dot(a, b, ca, cb):
@@ -37,8 +37,8 @@
 def kernel(
     q_ref, k_ref, v_ref, ct_ref, gate_hbm, vis_ref,
     qg_ref, kg_ref, vg_ref, gg_ref,
-    qw, cw, kv, obuf, rbuf, kvw, sg_ref, low_ref, both_ref, dqs, fin, gpart, gall, gsum, first, gate_ref, vis_s, slot_s,
-    ssem, rsem, hsend, hrecv, hout, lsem, lout, lfirst, esend, erecv, elocal, gsend, grecv, glast,
+    qw, cw, kv, obuf, rbuf, kvw, sg_ref, low_ref, both_ref, dqs, fin, gpart, gall, gsum, first, gate_ref, qct, kvt, dq_in, fin_in, gate_in, vis_s, slot_s,
+    ssem, rsem, hsend, hrecv, hout, lsem, lout, lfirst, lstage, lland, esend, erecv, elocal, gsend, grecv, glast,
 ):
     seq = lax.axis_index("seq")
     c, k = lax.div(seq, 2), lax.rem(seq, 2)
@@ -128,10 +128,16 @@
 
     def head_message(idx, h):
         g, n = h, 0
-        theirs = head_cols(1 - k, h)
-        if idx == IN_K:
-            return swap(idx, h, k_ref.at[:, theirs], kv.at[g, seq, 0, n])
-        return swap(idx, h, v_ref.at[:, theirs], kv.at[g, seq, 1, n])
+        theirs = head_cols(0, h)
+        if idx == DQ:
+            return swap_all(DQ, dqs.at[their_rows, theirs], dq_in.at[:, theirs])
+        if idx == OUT:
+            return swap_all(OUT, fin.at[1 - k, :, :, theirs], fin_in.at[:, :, theirs])
+        if idx == IN_Q:
+            return swap(idx, h, qct.at[0, :, theirs], qw.at[my_rows, theirs])
+        if idx == IN_C:
+            return swap(idx, h, qct.at[1, :, theirs], cw.at[my_rows, theirs])
+        return swap(idx, h, kvt.at[idx - IN_K, :, theirs], kv.at[g, seq, idx - IN_K, n])
 
     def head_got(idx, h, dst):
         swap(idx, h, dst, dst).wait_recv()
@@ -159,16 +165,10 @@
         results = ((1, fin.at[k, 0], kg_ref), (2, fin.at[k, 1], vg_ref))
         return [
             pltpu.make_async_copy(src, ref.at[:, half_cols], lout.at[i]) for i, src, ref in results
-        ] + [
-            swap_all(OUT_K, fin.at[1 - k, 0], kg_ref.at[:, half_cols]),
-            swap_all(OUT_V, fin.at[1 - k, 1], vg_ref.at[:, half_cols]),
         ]
 
-    def query_copies():
-        return [
-            pltpu.make_async_copy(dqs.at[my_rows], qg_ref.at[:, half_cols], lout.at[0]),
-            swap_all(DQ, dqs.at[their_rows], qg_ref.at[:, half_cols]),
-        ]
+    def query_copy():
+        return pltpu.make_async_copy(dqs.at[my_rows], qg_ref.at[:, half_cols], lout.at[0])
 
     def early(i, src, dst):
         return pltpu.make_async_remote_copy(
@@ -178,8 +178,12 @@
 
     swaps = [
         early(0, vis_ref, vis_s.at[k]),
-        early(1, q_ref.at[:, their_cols], qw.at[my_rows]),
-        early(2, ct_ref.at[:, their_cols], cw.at[my_rows]),
+    ]
+    theirs_staged = [
+        pltpu.make_async_copy(k_ref.at[:, their_cols], kvt.at[0], lstage.at[0]),
+        pltpu.make_async_copy(v_ref.at[:, their_cols], kvt.at[1], lstage.at[1]),
+        pltpu.make_async_copy(q_ref.at[:, their_cols], qct.at[0], lstage.at[2]),
+        pltpu.make_async_copy(ct_ref.at[:, their_cols], qct.at[1], lstage.at[3]),
     ]
     keeps = [
         pltpu.make_async_copy(vis_ref, vis_s.at[k], elocal.at[0]),
@@ -229,7 +233,7 @@
         for copy in own_copies(h):
             copy.start()
 
-    for copy in keeps:
+    for copy in theirs_staged + keeps:
         copy.start()
 
     barrier = pltpu.get_barrier_semaphore()
@@ -240,9 +244,11 @@
 
     send_first()
 
+    for copy in theirs_staged:
+        copy.wait()
     for h in range(AHEAD):
-        head_message(IN_K, h).start()
-        head_message(IN_V, h).start()
+        for idx in (IN_K, IN_V, IN_Q, IN_C):
+            head_message(idx, h).start()
 
     for copy in swaps:
         copy.start()
@@ -342,6 +348,11 @@
         head_got(IN_K, g, kv.at[g, other, 0, 0])
         head_got(IN_V, g, kv.at[g, other, 1, 0])
 
+    def swapped_queries(g):
+        theirs = head_cols(0, g)
+        head_got(IN_Q, g, qw.at[their_rows, theirs])
+        head_got(IN_C, g, cw.at[their_rows, theirs])
+
     def gather1(g):
         for copy in own_copies(g):
             copy.wait()
@@ -502,6 +513,8 @@
             def _():
                 finish(())
 
+        head_message(OUT, g).start()
+
     odd = lax.rem(x, 2)
     pairs = (
         across,
@@ -517,9 +530,15 @@
 
     gate_local = pltpu.make_async_copy(gsum.at[3], gg_ref.at[k], glast.at[0])
     gate_remote = pltpu.make_async_remote_copy(
-        src_ref=gsum.at[3], dst_ref=gg_ref.at[k], send_sem=glast.at[1], recv_sem=glast.at[2],
+        src_ref=gsum.at[3], dst_ref=gate_in, send_sem=glast.at[1], recv_sem=glast.at[2],
         device_id=partner, device_id_type=MESH,
     )
+    landed = [
+        pltpu.make_async_copy(dq_in, qg_ref.at[:, their_cols], lland.at[0]),
+        pltpu.make_async_copy(fin_in.at[0], kg_ref.at[:, their_cols], lland.at[1]),
+        pltpu.make_async_copy(fin_in.at[1], vg_ref.at[:, their_cols], lland.at[2]),
+        pltpu.make_async_copy(gate_in, gg_ref.at[1 - k], lland.at[3]),
+    ]
 
     def iteration(t):
         fixed = isinstance(t, int)
@@ -542,8 +561,8 @@
         def fetch(g):
             for copy in own_copies(g):
                 copy.start()
-            head_message(IN_K, g).start()
-            head_message(IN_V, g).start()
+            for idx in (IN_K, IN_V, IN_Q, IN_C):
+                head_message(idx, g).start()
 
         stage(-AHEAD, lambda g: fetch(g))
         stage(0, gather1, 1)
@@ -555,9 +574,11 @@
         stage(LAST, back4)
         if not fixed:
             gather4(t - COMPUTE)
+            swapped_queries(t - COMPUTE)
             span_work(t - COMPUTE)
         stage(GATHER3, gather3)
         if not fixed:
+            head_message(DQ, t - COMPUTE).start()
             products(t - COMPUTE)
             back1(t - COMPUTE)
 
@@ -571,8 +592,7 @@
     def _(t):
         iteration(t)
 
-    for copy in query_copies():
-        copy.start()
+    query_copy().start()
     gsum[0] = gpart[...]
     gate_step(0).start()
     for i in range(LAST - COMPUTE):
@@ -588,6 +608,14 @@
 
     for copy in result_copies():
         copy.start()
+    swap_all(DQ, dqs.at[their_rows], dq_in).wait_recv()
+    landed[0].start()
+    gate_remote.wait_recv()
+    landed[3].start()
+    swap_all(OUT, fin.at[1 - k], fin_in).wait_recv()
+    landed[1].start()
+    landed[2].start()
+
     for i in range(3):
         gate_step(i).wait_send()
 
@@ -641,23 +669,21 @@
     def _():
         done(R_R)
 
-    swap_all(DQ, dqs.at[their_rows], qg_ref.at[:, their_cols]).wait_send()
-    swap_all(OUT_K, fin.at[1 - k, 0], kg_ref.at[:, their_cols]).wait_send()
-    swap_all(OUT_V, fin.at[1 - k, 1], vg_ref.at[:, their_cols]).wait_send()
-    swap_all(IN_K, k_ref.at[:, their_cols], kg_ref.at[:, their_cols]).wait_send()
-    swap_all(IN_V, v_ref.at[:, their_cols], vg_ref.at[:, their_cols]).wait_send()
-    for idx, ref in ((DQ, qg_ref), (OUT_K, kg_ref), (OUT_V, vg_ref)):
-        swap_all(idx, ref.at[:, their_cols], ref.at[:, their_cols]).wait_recv()
+    swap_all(DQ, dqs.at[their_rows], dq_in).wait_send()
+    swap_all(OUT, fin.at[1 - k], fin_in).wait_send()
+    for idx, sent in ((IN_K, kvt.at[0]), (IN_V, kvt.at[1]), (IN_Q, qct.at[0]), (IN_C, qct.at[1])):
+        pltpu.make_async_remote_copy(
+            src_ref=sent, dst_ref=sent, send_sem=hsend.at[idx], recv_sem=hout.at[0],
+            device_id=partner, device_id_type=MESH,
+        ).wait_send()
+    for copy in landed:
+        copy.wait()
     pltpu.make_async_copy(qg_ref.at[:, half_cols], qg_ref.at[:, half_cols], lout.at[0]).wait()
     pltpu.make_async_copy(kg_ref.at[:, half_cols], kg_ref.at[:, half_cols], lout.at[1]).wait()
     pltpu.make_async_copy(vg_ref.at[:, half_cols], vg_ref.at[:, half_cols], lout.at[2]).wait()
 
     gate_local.wait()
     gate_remote.wait_send()
-    pltpu.make_async_remote_copy(
-        src_ref=gsum.at[3], dst_ref=gg_ref.at[1 - k], send_sem=glast.at[1], recv_sem=glast.at[2],
-        device_id=partner, device_id_type=MESH,
-    ).wait_recv()
 
 
 def place(a0, a1, a2, a3, b0, b1, b2, b3, m0, m1, m2, m3, sem):
@@ -711,16 +737,23 @@
             pltpu.VMEM((4, CORE_HEADS, D), F32),
             pltpu.VMEM((1, 2, N, LAT, D), BF16),
             pltpu.VMEM((2 * CORE_HEADS, D), F32),
+            pltpu.VMEM((2, tokens, half), BF16),
+            pltpu.VMEM((2, LAT, half), BF16),
+            pltpu.VMEM((tokens, half), BF16),
+            pltpu.VMEM((2, LAT, half), BF16),
+            pltpu.VMEM((CORE_HEADS, D), F32),
             pltpu.SMEM((2, 2, VIS), jnp.int32),
             pltpu.SMEM((4, IMAGES), jnp.int32),
             dma((MESSAGES,)),
             dma((CHUNKS, MESSAGES)),
-            dma((5,)),
-            dma((CORE_HEADS, 2)),
-            dma((3,)),
+            dma((6,)),
+            dma((CORE_HEADS, 4)),
+            dma((2,)),
             dma((CORE_HEADS, 2)),
             dma((3,)),
             dma((2,)),
+            dma((4,)),
+            dma((4,)),
             dma((3,)),
             dma((3,)),
             dma((4,)),

time: 68.5 us -> 69.1 us (level)
  no operation moved by 1% of the time
where the time goes in v2:
time: 69.1 us; the launch traced here: 68.9 us
  Pallas kernels  68.3 us (99%)
    pallas_call x1, Pallas kernels, shards(): pl.pallas_call(kernel, out_shape=out_shape, in_specs=[hbm_spec] * 6, out_...  65.9 us
    pallas_call x1, Pallas kernels, shards(): pl.pallas_call(place, out_shape=out_shape, in_specs=[any_spec] * 4, out_s...  2.43 us

profile of v2, /device:TPU:1, one launch (start us, length us, event | category | flops | bytes accessed | tf_op | source)
XLA Modules:
  0.0 68.9 jit_solution(8248954060335810608)
XLA Ops:
  0.6 65.9 %cross_attention_backward.1 = (bf16[256,2048]{1,0:T(8,128)(2,1)}, bf16[64,2048]{1,0:T(8,128)(2,1)}, bf16[64,2048]{1,0:T(8,128)(2,1)}, f32[2,8,128]{2,1,0:T(8,128)}) custom-call(bf16[256,2048]{1,0:T(8,128)(2,1)} %q_ref.1, bf16[64,2048]{1,0:T(8,128)(2,1)} %k_ref.1, bf16[64,2048]{1,0:T(8,128)(2,1)} %v_ref.1, bf16[256,2048]{1,0:T(8,128)(2,1)} %ct_ref.1, ...), custom_call_target="tpu_custom_call" | custom-call | tf_op jit(solution)/shard_map/cross_attention_backward/pallas_call | solution.py:718
  66.5 2.4 %place_results.1 = (bf16[256,2048]{1,0:T(8,128)(2,1)}, bf16[64,2048]{1,0:T(8,128)(2,1)}, bf16[64,2048]{1,0:T(8,128)(2,1)}, f32[2,8,128]{2,1,0:T(8,128)}) custom-call(bf16[256,2048]{1,0:T(8,128)(2,1)} %get-tuple-element.12.a0, bf16[64,2048]{1,0:T(8,128)(2,1)} %get-tuple-element.13.a1, bf16[64,2048]{1,0:T(8,128)(2,1)} %get-tuple-element.14.a2, ...), custom_call_target="tpu_custom_call" | custom-call | tf_op jit(solution)/shard_map/place_results/pallas_call | solution.py:769

commit v3 on v2

--- a/solution.py
+++ b/solution.py
@@ -15,7 +15,8 @@
 CORE_HEADS = 8
 N = 1
 CHUNKS = CORE_HEADS // N
-AHEAD = 2
+AHEAD = 6
+EARLY = 6
 IMAGES = 16
 GATHER2, GATHER3, COMPUTE, BACK2, BACK3, LAST = 1, 2, 3, 5, 7, 9
 NEG = -1e30
@@ -37,7 +38,7 @@
 def kernel(
     q_ref, k_ref, v_ref, ct_ref, gate_hbm, vis_ref,
     qg_ref, kg_ref, vg_ref, gg_ref,
-    qw, cw, kv, obuf, rbuf, kvw, sg_ref, low_ref, both_ref, dqs, fin, gpart, gall, gsum, first, gate_ref, qct, kvt, dq_in, fin_in, gate_in, vis_s, slot_s,
+    qw, cw, kv, obuf, rbuf, kvw, sg_ref, low_ref, both_ref, q_turned, go_turned, dqs, fin, gpart, gall, gsum, first, gate_ref, qct, kvt, dq_in, fin_in, gate_in, vis_s, slot_s,
     ssem, rsem, hsend, hrecv, hout, lsem, lout, lfirst, lstage, lland, esend, erecv, elocal, gsend, grecv, glast,
 ):
     seq = lax.axis_index("seq")
@@ -273,24 +274,29 @@
     def when(cond):
         return pl.when(cond)
 
+    def text_work(h):
+        swapped_queries(h)
+        cols = pl.ds(h * D if isinstance(h, int) else pl.multiple_of(h * D, D), D)
+        tanh_gate = jnp.tanh(gate_ref[pl.ds(k * CORE_HEADS + h, 1), :])
+        ct_all = cw[:, cols]
+        go_all = (tanh_gate * ct_all.astype(F32)).astype(BF16)
+        both_ref[h, :, :D] = go_all
+        both_ref[h, :, D:] = ct_all
+        for s in range(4):
+            rows = pl.ds(s * SPAN, SPAN)
+            q_turned[h, s] = qw[rows, cols].T
+            go_turned[h, s] = go_all[s * SPAN : (s + 1) * SPAN].T
+
     def span_work(h):
         cols = pl.ds(pl.multiple_of(h * D, D), D)
         kvw[...] = kv[h, :, :, 0]
-        tanh_gate = jnp.tanh(gate_ref[pl.ds(k * CORE_HEADS + h, 1), :])
-        q_all = qw[:, cols]
-        ct_all = cw[:, cols]
-        go_all = (tanh_gate * ct_all.astype(F32)).astype(BF16)
-        both_ref[:, :D] = go_all
-        both_ref[:, D:] = ct_all
         spans = range(4)
         listed = [[vis_s[s // 2, s % 2, v] for v in range(VIS)] for s in spans]
         ids = [[jnp.maximum(i, 0) for i in row] for row in listed]
-        q = [q_all[s * SPAN : (s + 1) * SPAN] for s in spans]
-        go = [go_all[s * SPAN : (s + 1) * SPAN] for s in spans]
         kl = [jnp.concatenate([kvw[i, 0] for i in ids[s]], axis=0) for s in spans]
         vl = [jnp.concatenate([kvw[i, 1] for i in ids[s]], axis=0) for s in spans]
-        raw = [dot(kl[s], q[s], 1, 1) for s in spans]
-        wg = [dot(vl[s], go[s], 1, 1) for s in spans]
+        raw = [dot(kl[s], q_turned[h, s], 1, 0) for s in spans]
+        wg = [dot(vl[s], go_turned[h, s], 1, 0) for s in spans]
         p, low, sg = [], [], []
         for s in spans:
             rows = [raw[s][:LAT] * EXP2_SCALE]
@@ -314,7 +320,7 @@
     def products(g):
         tanh_gate = jnp.tanh(gate_ref[pl.ds(k * CORE_HEADS + g, 1), :])
         q_all = qw[:, pl.ds(pl.multiple_of(g * D, D), D)]
-        both = both_ref[...]
+        both = both_ref[g]
 
         def images(count):
             left, low_left, vals = [], [], []
@@ -573,8 +579,8 @@
         stage(BACK3, back3)
         stage(LAST, back4)
         if not fixed:
+            pl.when(t - COMPUTE < CHUNKS - EARLY)(lambda: text_work(t - COMPUTE + EARLY))
             gather4(t - COMPUTE)
-            swapped_queries(t - COMPUTE)
             span_work(t - COMPUTE)
         stage(GATHER3, gather3)
         if not fixed:
@@ -582,10 +588,15 @@
             products(t - COMPUTE)
             back1(t - COMPUTE)
 
-    for t in range(COMPUTE - 1):
-        iteration(t)
+    iteration(0)
     prepare()
-    iteration(COMPUTE - 1)
+    text_work(0)
+    iteration(1)
+    for h in range(1, EARLY - 2):
+        text_work(h)
+    iteration(2)
+    for h in range(EARLY - 2, EARLY):
+        text_work(h)
     swapped(0)
 
     @pl.loop(COMPUTE, COMPUTE + CHUNKS)
@@ -729,7 +740,9 @@
             pltpu.VMEM((IMAGES, 2, LAT, D), BF16),
             pltpu.VMEM((4, VIS + 1, LAT, SPAN), BF16),
             pltpu.VMEM((4, VIS + 1, LAT, SPAN), BF16),
-            pltpu.VMEM((2 * tokens, 2 * D), BF16),
+            pltpu.VMEM((CORE_HEADS, 2 * tokens, 2 * D), BF16),
+            pltpu.VMEM((CORE_HEADS, 4, D, SPAN), BF16),
+            pltpu.VMEM((CORE_HEADS, 4, D, SPAN), BF16),
             pltpu.VMEM((2 * tokens, half), BF16),
             pltpu.VMEM((2, 2, LAT, half), BF16),
             pltpu.VMEM((CORE_HEADS, D), F32),

time: 69.1 us -> 68.8 us (level)
  no operation moved by 1% of the time
where the time goes in v3:
time: 68.8 us; the launch traced here: 68.6 us
  Pallas kernels  68 us (99%)
    pallas_call x1, Pallas kernels, shards(): pl.pallas_call(kernel, out_shape=out_shape, in_specs=[hbm_spec] * 6, out_...  65.6 us
    pallas_call x1, Pallas kernels, shards(): pl.pallas_call(place, out_shape=out_shape, in_specs=[any_spec] * 4, out_s...  2.43 us

profile of v3, /device:TPU:1, one launch (start us, length us, event | category | flops | bytes accessed | tf_op | source)
XLA Modules:
  0.0 68.6 jit_solution(9877073614909970132)
XLA Ops:
  0.6 65.6 %cross_attention_backward.1 = (bf16[256,2048]{1,0:T(8,128)(2,1)}, bf16[64,2048]{1,0:T(8,128)(2,1)}, bf16[64,2048]{1,0:T(8,128)(2,1)}, f32[2,8,128]{2,1,0:T(8,128)}) custom-call(bf16[256,2048]{1,0:T(8,128)(2,1)} %q_ref.1, bf16[64,2048]{1,0:T(8,128)(2,1)} %k_ref.1, bf16[64,2048]{1,0:T(8,128)(2,1)} %v_ref.1, bf16[256,2048]{1,0:T(8,128)(2,1)} %ct_ref.1, ...), custom_call_target="tpu_custom_call" | custom-call | tf_op jit(solution)/shard_map/cross_attention_backward/pallas_call | solution.py:729
  66.2 2.4 %place_results.1 = (bf16[256,2048]{1,0:T(8,128)(2,1)}, bf16[64,2048]{1,0:T(8,128)(2,1)}, bf16[64,2048]{1,0:T(8,128)(2,1)}, f32[2,8,128]{2,1,0:T(8,128)}) custom-call(bf16[256,2048]{1,0:T(8,128)(2,1)} %get-tuple-element.12.a0, bf16[64,2048]{1,0:T(8,128)(2,1)} %get-tuple-element.13.a1, bf16[64,2048]{1,0:T(8,128)(2,1)} %get-tuple-element.14.a2, ...), custom_call_target="tpu_custom_call" | custom-call | tf_op jit(solution)/shard_map/place_results/pallas_call | solution.py:782

commit v4 on v2

--- a/solution.py
+++ b/solution.py
@@ -24,9 +24,10 @@
 
 (
     A_R, A_L, A_FR, A_FL, A_Z0, A_ZM, A_ZP, A_HR, A_HL,
-    R_R, R_L, R_FR, R_FL, R_Z0, R_ZM, R_ZP, R_HR, R_HL,
-) = range(18)
-MESSAGES = 18
+    R_R, R_L, R_L2, R_FR, R_Z0, R_ZM, R_ZP, R_HR, R_HL, R_HO,
+) = range(19)
+MESSAGES = 19
+HALVES = (A_HR, A_HL, R_L, R_L2, R_ZP, R_HR, R_HL, R_HO)
 DQ, OUT, IN_K, IN_V, IN_Q, IN_C = range(6)
 
 
@@ -65,6 +66,9 @@
 
     def img(buf, g, b, half):
         return buf.at[g, pl.ds(2 * b + half, 1)]
+
+    def rhalf(g, slot, half):
+        return rbuf.at[g, slot, pl.ds(half, 1)]
 
     hi = z * 4
 
@@ -97,21 +101,23 @@
         if idx == R_R:
             return send(idx, g, blk(obuf, g, hi + xl), rbuf.at[g, 0], left)
         if idx == R_L:
-            return send(idx, g, blk(obuf, g, hi + xr), rbuf.at[g, 1], right)
+            return send(idx, g, img(obuf, g, hi + xr, 0), rhalf(g, 1, 0), right)
+        if idx == R_L2:
+            return send(idx, g, img(obuf, g, hi + xr, 1), rhalf(g, 1, 1), right)
         if idx == R_FR:
             return send(idx, g, blk(obuf, g, hi + xo), rbuf.at[g, 2], left)
-        if idx == R_FL:
-            return send(idx, g, blk(obuf, g, hi + xo), rbuf.at[g, 3], right)
         if idx == R_Z0:
             return send(idx, g, blk(obuf, g, x), rbuf.at[g, 4], across)
         if idx == R_ZM:
             return send(idx, g, blk(obuf, g, xl), rbuf.at[g, 5], across)
         if idx == R_ZP:
-            return send(idx, g, blk(obuf, g, xr), rbuf.at[g, 6], across)
+            return send(idx, g, img(obuf, g, xr, 0), rhalf(g, 6, 0), across)
         if idx == R_HR:
-            return send(idx, g, img(obuf, g, xo, 0), rbuf.at[g, 7, pl.ds(0, 1)], left)
+            return send(idx, g, img(obuf, g, xo, 1), rhalf(g, 3, 1), left)
         if idx == R_HL:
-            return send(idx, g, img(obuf, g, xo, 1), rbuf.at[g, 7, pl.ds(1, 1)], right)
+            return send(idx, g, img(obuf, g, xo, 0), rhalf(g, 3, 0), right)
+        if idx == R_HO:
+            return send(idx, g, img(obuf, g, xr, 1), rhalf(g, 6, 1), right)
         raise ValueError(idx)
 
     def swap(idx, h, src, dst):
@@ -418,20 +424,26 @@
         def _():
             got(A_L, g, blk(kv, g, 4))
 
+    def add_half(g, b, slot, half):
+        row = 2 * b + half
+        obuf[g, row] = (obuf[g, row].astype(F32) + rbuf[g, slot, half].astype(F32)).astype(BF16)
+
+    middle = jnp.logical_or(x == 1, x == 2)
+
     def back1(g):
         @when(z1)
         def _():
+            message(R_HO, g).start()
             message(R_HR, g).start()
             message(R_HL, g).start()
-            message(R_Z0, g).start()
-
-        @when(jnp.logical_or(x == 2, jnp.logical_and(z1, x == 3)))
+
+        @when(x >= 2)
         def _():
             message(R_FR, g).start()
 
-        @when(jnp.logical_and(z0, x == 3))
-        def _():
-            message(R_FL, g).start()
+        @when(x == 3)
+        def _():
+            message(R_L2, g).start()
 
         @when(jnp.logical_and(z1, x == 3))
         def _():
@@ -440,16 +452,17 @@
     def back2(g):
         @when(z1)
         def _():
-            got(R_HR, g, rbuf.at[g, 7, pl.ds(0, 1)])
-            row = 2 * xl
-            obuf[g, row] = (obuf[g, row].astype(F32) + rbuf[g, 7, 0].astype(F32)).astype(BF16)
+            got(R_HR, g, rhalf(g, 3, 1))
+            add_half(g, xl, 3, 1)
             message(R_ZM, g).start()
-            got(R_HL, g, rbuf.at[g, 7, pl.ds(1, 1)])
-            row = 2 * xr + 1
-            obuf[g, row] = (obuf[g, row].astype(F32) + rbuf[g, 7, 1].astype(F32)).astype(BF16)
+            got(R_HL, g, rhalf(g, 3, 0))
+            add_half(g, xr, 3, 0)
             message(R_ZP, g).start()
-
-            @when(jnp.logical_or(x == 1, x == 2))
+            got(R_HO, g, rhalf(g, 6, 1))
+            add_half(g, x, 6, 1)
+            message(R_Z0, g).start()
+
+            @when(middle)
             def _():
                 got(R_FR, g, rbuf.at[g, 2])
                 add(g, 4 + xl, 2)
@@ -461,29 +474,22 @@
     def back3(g):
         @when(z0)
         def _():
-            @when(x == 1)
+            @when(middle)
             def _():
                 got(R_FR, g, rbuf.at[g, 2])
                 add(g, xl, 2)
 
-            @when(x == 0)
-            def _():
-                got(R_FL, g, rbuf.at[g, 3])
-                add(g, xr, 3)
-
             got(R_ZM, g, rbuf.at[g, 5])
             add(g, xl, 5)
             message(R_R, g).start()
-            got(R_ZP, g, rbuf.at[g, 6])
-            add(g, xr, 6)
+            got(R_ZP, g, rhalf(g, 6, 0))
+            add_half(g, xr, 6, 0)
             message(R_L, g).start()
 
     def back4(g):
-        own = pl.ds(2 * c, 2)
-
-        def finish(slots):
-            total = obuf[g, own].astype(F32)
-            for slot in slots:
+        def finish(*whole):
+            total = obuf[g, pl.ds(2 * c, 2)].astype(F32)
+            for slot in whole:
                 total += rbuf[g, slot].astype(F32)
             fin[:, :, :, pl.ds(pl.multiple_of(g * D, D), D)] = total[:, :, 0].astype(BF16)
 
@@ -491,8 +497,17 @@
         def _():
             got(R_Z0, g, rbuf.at[g, 4])
             got(R_R, g, rbuf.at[g, 0])
-            got(R_L, g, rbuf.at[g, 1])
-            finish((4, 0, 1))
+            got(R_L, g, rhalf(g, 1, 0))
+
+            @when(x > 0)
+            def _():
+                add_half(g, c, 1, 0)
+                finish(4, 0)
+
+            @when(x == 0)
+            def _():
+                got(R_L2, g, rhalf(g, 1, 1))
+                finish(4, 0, 1)
 
         @when(z1)
         def _():
@@ -502,16 +517,17 @@
 
             @when(x == 0)
             def _():
-                got(R_L, g, rbuf.at[g, 1])
-                finish((0, 1))
-
-            @when(jnp.logical_or(x == 1, x == 2))
+                got(R_L, g, rhalf(g, 1, 0))
+                got(R_L2, g, rhalf(g, 1, 1))
+                finish(0, 1)
+
+            @when(middle)
             def _():
-                finish((0,))
+                finish(0)
 
             @when(x == 3)
             def _():
-                finish(())
+                finish()
 
         head_message(OUT, g).start()
 
@@ -619,23 +635,21 @@
     for i in range(3):
         gate_step(i).wait_send()
 
-    def done(idx):
-        half = idx in (A_HR, A_HL, R_HR, R_HL)
-        sent = kv.at[:, pl.ds(0, 1 if half else 2)]
-        pltpu.make_async_remote_copy(
-            src_ref=sent, dst_ref=sent, send_sem=ssem.at[idx], recv_sem=rsem.at[0, idx],
-            device_id=partner, device_id_type=MESH,
-        ).wait_send()
+    def done(*kinds):
+        for idx in kinds:
+            sent = kv.at[:, pl.ds(0, 1 if idx in HALVES else 2)]
+            pltpu.make_async_remote_copy(
+                src_ref=sent, dst_ref=sent, send_sem=ssem.at[idx], recv_sem=rsem.at[0, idx],
+                device_id=partner, device_id_type=MESH,
+            ).wait_send()
 
     @when(z0)
     def _():
-        for idx in (A_Z0, A_ZM, A_ZP):
-            done(idx)
+        done(A_Z0, A_ZM, A_ZP)
 
     @when(z1)
     def _():
-        for idx in (A_HR, A_HL, R_HR, R_HL, R_Z0, R_ZM, R_ZP):
-            done(idx)
+        done(A_HR, A_HL, R_HR, R_HL, R_HO, R_Z0, R_ZM, R_ZP)
 
     @when(jnp.logical_or(z0, x < 3))
     def _():
@@ -653,13 +667,13 @@
     def _():
         done(A_FL)
 
-    @when(jnp.logical_or(x == 2, jnp.logical_and(z1, x == 3)))
+    @when(x >= 2)
     def _():
         done(R_FR)
 
-    @when(jnp.logical_and(z0, x == 3))
-    def _():
-        done(R_FL)
+    @when(x == 3)
+    def _():
+        done(R_L2)
 
     @when(jnp.logical_or(z0, x == 3))
     def _():
@@ -725,7 +739,7 @@
             pltpu.VMEM((2 * tokens, half), BF16),
             pltpu.VMEM((CHUNKS, IMAGES, 2, N, LAT, D), BF16),
             pltpu.VMEM((CHUNKS, IMAGES, 2, N, LAT, D), BF16),
-            pltpu.VMEM((CHUNKS, 8, 2, 2, N, LAT, D), BF16),
+            pltpu.VMEM((CHUNKS, 7, 2, 2, N, LAT, D), BF16),
             pltpu.VMEM((IMAGES, 2, LAT, D), BF16),
             pltpu.VMEM((4, VIS + 1, LAT, SPAN), BF16),
             pltpu.VMEM((4, VIS + 1, LAT, SPAN), BF16),

time: 69.1 us -> 68.3 us (0.988)
  Pallas kernels: 68.3 us -> 67.6 us
    pallas_call x1, Pallas kernels: 65.9 us -> 65.1 us  [shards(): pl.pallas_call(kernel, out_shape=out_shape, in_specs=[hbm_spec] * 6, out_...]
where the time goes in v4:
time: 68.3 us; the launch traced here: 68.2 us
  Pallas kernels  67.6 us (99%)
    pallas_call x1, Pallas kernels, shards(): pl.pallas_call(kernel, out_shape=out_shape, in_specs=[hbm_spec] * 6, out_...  65.1 us
    pallas_call x1, Pallas kernels, shards(): pl.pallas_call(place, out_shape=out_shape, in_specs=[any_spec] * 4, out_s...  2.43 us

profile of v4, /device:TPU:1, one launch (start us, length us, event | category | flops | bytes accessed | tf_op | source)
XLA Modules:
  0.0 68.2 jit_solution(16574468106555613978)
XLA Ops:
  0.6 65.1 %cross_attention_backward.1 = (bf16[256,2048]{1,0:T(8,128)(2,1)}, bf16[64,2048]{1,0:T(8,128)(2,1)}, bf16[64,2048]{1,0:T(8,128)(2,1)}, f32[2,8,128]{2,1,0:T(8,128)}) custom-call(bf16[256,2048]{1,0:T(8,128)(2,1)} %q_ref.1, bf16[64,2048]{1,0:T(8,128)(2,1)} %k_ref.1, bf16[64,2048]{1,0:T(8,128)(2,1)} %v_ref.1, bf16[256,2048]{1,0:T(8,128)(2,1)} %ct_ref.1, ...), custom_call_target="tpu_custom_call" | custom-call | tf_op jit(solution)/shard_map/cross_attention_backward/pallas_call | solution.py:732
  65.8 2.4 %place_results.1 = (bf16[256,2048]{1,0:T(8,128)(2,1)}, bf16[64,2048]{1,0:T(8,128)(2,1)}, bf16[64,2048]{1,0:T(8,128)(2,1)}, f32[2,8,128]{2,1,0:T(8,128)}) custom-call(bf16[256,2048]{1,0:T(8,128)(2,1)} %get-tuple-element.12.a0, bf16[64,2048]{1,0:T(8,128)(2,1)} %get-tuple-element.13.a1, bf16[64,2048]{1,0:T(8,128)(2,1)} %get-tuple-element.14.a2, ...), custom_call_target="tpu_custom_call" | custom-call | tf_op jit(solution)/shard_map/place_results/pallas_call | solution.py:783

commit v5 on v4

--- a/solution.py
+++ b/solution.py
@@ -580,12 +580,12 @@
             for idx in (IN_K, IN_V, IN_Q, IN_C):
                 head_message(idx, g).start()
 
+        stage(BACK2, back2)
         stage(-AHEAD, lambda g: fetch(g))
         stage(0, gather1, 1)
         stage(GATHER2, gather2)
         stage(0, gather_own, 1)
         stage(GATHER2, gather_forward)
-        stage(BACK2, back2)
         stage(BACK3, back3)
         stage(LAST, back4)
         if not fixed:
@@ -701,13 +701,10 @@
 
 
 def place(a0, a1, a2, a3, b0, b1, b2, b3, m0, m1, m2, m3, sem):
-    held = (m0, m1, m2, m3)
-    into = [
-        pltpu.make_async_copy(a, m, sem.at[0, i]) for i, (a, m) in enumerate(zip((a0, a1, a2, a3), held))
-    ]
-    out = [
-        pltpu.make_async_copy(m, b, sem.at[1, i]) for i, (m, b) in enumerate(zip(held, (b0, b1, b2, b3)))
-    ]
+    pieces = [(a0.at[r], m0.at[r], b0.at[r]) for r in (pl.ds(64 * i, 64) for i in range(4))]
+    pieces += [(a1, m1, b1), (a2, m2, b2), (a3, m3, b3)]
+    into = [pltpu.make_async_copy(a, m, sem.at[0, i]) for i, (a, m, _) in enumerate(pieces)]
+    out = [pltpu.make_async_copy(m, b, sem.at[1, i]) for i, (_, m, b) in enumerate(pieces)]
     for copy in into:
         copy.start()
     for copy, after in zip(into, out):
@@ -785,7 +782,7 @@
         out_shape=out_shape,
         in_specs=[any_spec] * 4,
         out_specs=(hbm_spec,) * 4,
-        scratch_shapes=[pltpu.VMEM(o.shape, o.dtype) for o in out_shape] + [dma((2, 4))],
+        scratch_shapes=[pltpu.VMEM(o.shape, o.dtype) for o in out_shape] + [dma((2, 7))],
         compiler_params=pltpu.CompilerParams(vmem_limit_bytes=63 * 1024 * 1024),
         name="place_results",
     )(*results)

time: 68.3 us -> 68.1 us (level)
  no operation moved by 1% of the time
where the time goes in v5:
time: 68.1 us; the launch traced here: 68 us
  Pallas kernels  67.4 us (99%)
    pallas_call x1, Pallas kernels, shards(): pl.pallas_call(kernel, out_shape=out_shape, in_specs=[hbm_spec] * 6, out_...  65.2 us
    pallas_call x1, Pallas kernels, shards(): pl.pallas_call(place, out_shape=out_shape, in_specs=[any_spec] * 4, out_s...  2.21 us

profile of v5, /device:TPU:1, one launch (start us, length us, event | category | flops | bytes accessed | tf_op | source)
XLA Modules:
  0.0 68.0 jit_solution(9638946391790742483)
XLA Ops:
  0.6 65.2 %cross_attention_backward.1 = (bf16[256,2048]{1,0:T(8,128)(2,1)}, bf16[64,2048]{1,0:T(8,128)(2,1)}, bf16[64,2048]{1,0:T(8,128)(2,1)}, f32[2,8,128]{2,1,0:T(8,128)}) custom-call(bf16[256,2048]{1,0:T(8,128)(2,1)} %q_ref.1, bf16[64,2048]{1,0:T(8,128)(2,1)} %k_ref.1, bf16[64,2048]{1,0:T(8,128)(2,1)} %v_ref.1, bf16[256,2048]{1,0:T(8,128)(2,1)} %ct_ref.1, ...), custom_call_target="tpu_custom_call" | custom-call | tf_op jit(solution)/shard_map/cross_attention_backward/pallas_call | solution.py:729
  65.8 2.2 %place_results.1 = (bf16[256,2048]{1,0:T(8,128)(2,1)}, bf16[64,2048]{1,0:T(8,128)(2,1)}, bf16[64,2048]{1,0:T(8,128)(2,1)}, f32[2,8,128]{2,1,0:T(8,128)}) custom-call(bf16[256,2048]{1,0:T(8,128)(2,1)} %get-tuple-element.12.a0, bf16[64,2048]{1,0:T(8,128)(2,1)} %get-tuple-element.13.a1, bf16[64,2048]{1,0:T(8,128)(2,1)} %get-tuple-element.14.a2, ...), custom_call_target="tpu_custom_call" | custom-call | tf_op jit(solution)/shard_map/place_results/pallas_call | solution.py:780

commit v6 on v5

--- a/solution.py
+++ b/solution.py
@@ -581,12 +581,12 @@
                 head_message(idx, g).start()
 
         stage(BACK2, back2)
+        stage(BACK3, back3)
         stage(-AHEAD, lambda g: fetch(g))
         stage(0, gather1, 1)
         stage(GATHER2, gather2)
         stage(0, gather_own, 1)
         stage(GATHER2, gather_forward)
-        stage(BACK3, back3)
         stage(LAST, back4)
         if not fixed:
             gather4(t - COMPUTE)
@@ -613,6 +613,11 @@
     gate_step(0).start()
     for i in range(LAST - COMPUTE):
         iteration(COMPUTE + CHUNKS + i)
+        if i == 4:
+            swap_all(DQ, dqs.at[their_rows], dq_in).wait_recv()
+            landed[0].start()
+            gate_remote.wait_recv()
+            landed[3].start()
         if i < 3:
             gate_step(i).wait_recv()
             gsum[i + 1] = gsum[i] + gall[i]
@@ -624,10 +629,6 @@
 
     for copy in result_copies():
         copy.start()
-    swap_all(DQ, dqs.at[their_rows], dq_in).wait_recv()
-    landed[0].start()
-    gate_remote.wait_recv()
-    landed[3].start()
     swap_all(OUT, fin.at[1 - k], fin_in).wait_recv()
     landed[1].start()
     landed[2].start()

time: 68.1 us -> 68.1 us (level)
  no operation moved by 1% of the time
where the time goes in v6:
time: 68.1 us; the launch traced here: 68 us
  Pallas kernels  67.4 us (99%)
    pallas_call x1, Pallas kernels, shards(): pl.pallas_call(kernel, out_shape=out_shape, in_specs=[hbm_spec] * 6, out_...  65.2 us
    pallas_call x1, Pallas kernels, shards(): pl.pallas_call(place, out_shape=out_shape, in_specs=[any_spec] * 4, out_s...  2.21 us

profile of v6, /device:TPU:1, one launch (start us, length us, event | category | flops | bytes accessed | tf_op | source)
XLA Modules:
  0.0 68.0 jit_solution(2172078042237633764)
XLA Ops:
  0.6 65.2 %cross_attention_backward.1 = (bf16[256,2048]{1,0:T(8,128)(2,1)}, bf16[64,2048]{1,0:T(8,128)(2,1)}, bf16[64,2048]{1,0:T(8,128)(2,1)}, f32[2,8,128]{2,1,0:T(8,128)}) custom-call(bf16[256,2048]{1,0:T(8,128)(2,1)} %q_ref.1, bf16[64,2048]{1,0:T(8,128)(2,1)} %k_ref.1, bf16[64,2048]{1,0:T(8,128)(2,1)} %v_ref.1, bf16[256,2048]{1,0:T(8,128)(2,1)} %ct_ref.1, ...), custom_call_target="tpu_custom_call" | custom-call | tf_op jit(solution)/shard_map/cross_attention_backward/pallas_call | solution.py:730
  65.8 2.2 %place_results.1 = (bf16[256,2048]{1,0:T(8,128)(2,1)}, bf16[64,2048]{1,0:T(8,128)(2,1)}, bf16[64,2048]{1,0:T(8,128)(2,1)}, f32[2,8,128]{2,1,0:T(8,128)}) custom-call(bf16[256,2048]{1,0:T(8,128)(2,1)} %get-tuple-element.12.a0, bf16[64,2048]{1,0:T(8,128)(2,1)} %get-tuple-element.13.a1, bf16[64,2048]{1,0:T(8,128)(2,1)} %get-tuple-element.14.a2, ...), custom_call_target="tpu_custom_call" | custom-call | tf_op jit(solution)/shard_map/place_results/pallas_call | solution.py:781

commit v7 on v5

--- a/solution.py
+++ b/solution.py
@@ -15,7 +15,7 @@
 CORE_HEADS = 8
 N = 1
 CHUNKS = CORE_HEADS // N
-AHEAD = 2
+AHEAD = 8
 IMAGES = 16
 GATHER2, GATHER3, COMPUTE, BACK2, BACK3, LAST = 1, 2, 3, 5, 7, 9
 NEG = -1e30

time: 68.1 us -> 68.2 us (level)
  no operation moved by 1% of the time
where the time goes in v7:
time: 68.2 us; the launch traced here: 68.1 us
  Pallas kernels  67.4 us (99%)
    pallas_call x1, Pallas kernels, shards(): pl.pallas_call(kernel, out_shape=out_shape, in_specs=[hbm_spec] * 6, out_...  65.2 us
    pallas_call x1, Pallas kernels, shards(): pl.pallas_call(place, out_shape=out_shape, in_specs=[any_spec] * 4, out_s...  2.21 us

profile of v7, /device:TPU:1, one launch (start us, length us, event | category | flops | bytes accessed | tf_op | source)
XLA Modules:
  0.0 68.1 jit_solution(15065298427985737711)
XLA Ops:
  0.6 65.2 %cross_attention_backward.1 = (bf16[256,2048]{1,0:T(8,128)(2,1)}, bf16[64,2048]{1,0:T(8,128)(2,1)}, bf16[64,2048]{1,0:T(8,128)(2,1)}, f32[2,8,128]{2,1,0:T(8,128)}) custom-call(bf16[256,2048]{1,0:T(8,128)(2,1)} %q_ref.1, bf16[64,2048]{1,0:T(8,128)(2,1)} %k_ref.1, bf16[64,2048]{1,0:T(8,128)(2,1)} %v_ref.1, bf16[256,2048]{1,0:T(8,128)(2,1)} %ct_ref.1, ...), custom_call_target="tpu_custom_call" | custom-call | tf_op jit(solution)/shard_map/cross_attention_backward/pallas_call | solution.py:729
  65.9 2.2 %place_results.1 = (bf16[256,2048]{1,0:T(8,128)(2,1)}, bf16[64,2048]{1,0:T(8,128)(2,1)}, bf16[64,2048]{1,0:T(8,128)(2,1)}, f32[2,8,128]{2,1,0:T(8,128)}) custom-call(bf16[256,2048]{1,0:T(8,128)(2,1)} %get-tuple-element.12.a0, bf16[64,2048]{1,0:T(8,128)(2,1)} %get-tuple-element.13.a1, bf16[64,2048]{1,0:T(8,128)(2,1)} %get-tuple-element.14.a2, ...), custom_call_target="tpu_custom_call" | custom-call | tf_op jit(solution)/shard_map/place_results/pallas_call | solution.py:780
